TPU v7x, 32 devices: a whole 2x2x4 slice. The times are simulated.
32 devices in a mesh: leaf: 16 (over z, y, x), cols: 2 (over core).
Axes of the slice: x: 2, y: 2, z: 4, core: 2. Of those that a mesh axis runs over, the one named last changes fastest.
Arguments:
- vectors: bfloat16 [128, 32768], P('cols', 'leaf'), may hold values from -6 to 6
- near_blocks: bfloat16 [128, 8, 256, 256], P('leaf', None, 'cols'), may hold values from -0.125 to 0.125
- near_index: int32 [128, 8], P('leaf'), may hold values from -1 to 127, as said below
- far_index: int32 [128, 8], P('leaf'), may hold values from -1 to 127, as said below
- far_kind: int32 [128, 8], P('leaf'), may hold values from 0 to 15
- cluster_basis: bfloat16 [128, 64, 256], P('leaf'), may hold values from -0.375 to 0.375
- leaf_transfer: float32 [128, 64, 64], P('leaf'), may hold values from -0.25 to 0.25
- coupling_table: float32 [16, 64, 64], replicated, may hold values from -0.5 to 0.5
- parent_transfer_matrices: float32 [2, 64, 64], replicated, may hold values from -0.625 to 0.625
- coarse_kind: int32 [15], replicated, may hold values from 0 to 15
Outputs:
- product: bfloat16 [128, 32768], P('cols', 'leaf')
Inputs may be any that keep to these rules, and one draw needn't show every extreme that they name: `near_index`: row i holds distinct leaves within 8 positions of leaf i, and -1 in unused slots; its first entry is i itself, its second is i - 8 for even i and i + 8 for odd i, or -1 where that is outside the leaves. No leaf stands in both near_index and far_index of one row. `far_index`: row i holds distinct leaves other than i within 8 positions of leaf i, and -1 in unused slots.
All inputs are finite; a program needn't handle non-finite values.
Results may differ from a plain program's by a relative error of at most 0.0044.
Values may be sent and summed in bfloat16 or wider, within the bound.
A program may use at most 128 MiB of HBM per device.

v0:
```python
import jax
import jax.numpy as jnp
from jax import lax
from jax.sharding import PartitionSpec as P


def padded(array, sides, width):
    for axis, dim in sides:
        peers, length = (lax.axis_size(axis), array.shape[dim])
        up = [(i, (i + 1) % peers) for i in range(peers - 1)]
        down = [(j, i) for i, j in up]
        last = lax.slice_in_dim(array, length - width, length, axis=dim)
        leading = lax.slice_in_dim(array, 0, width, axis=dim)
        before = lax.ppermute(last, axis, up)
        after = lax.ppermute(leading, axis, down)
        array = jnp.concatenate([before, array, after], axis=dim)
    return array


def partner(block, axis, apart):
    count = lax.axis_size(axis)
    route = []
    for low in range(count):
        high = low | 1 << apart
        if high != low and high < count:
            route += [(low, high), (high, low)]
    return lax.ppermute(block, axis, route)


def shards(
    vectors,
    near_blocks,
    near_index,
    far_index,
    far_kind,
    cluster_basis,
    leaf_transfer,
    coupling_table,
    parent_transfer_matrices,
    coarse_kind,
):
    upper_level = lax.Precision.HIGHEST
    cols_here = vectors.shape[0]
    leaf_count = cluster_basis.shape[0]
    leaf_rows = cluster_basis.shape[2]
    device_index = lax.axis_index("leaf")
    groups = lax.axis_size("leaf")
    window_start = (device_index - 1) * leaf_count
    vector_leaves = vectors.reshape(cols_here, leaf_count, leaf_rows)
    leaf_coefs = jnp.einsum(
        "cir,iqr->icq", vector_leaves, cluster_basis, preferred_element_type=jnp.float32
    )
    group_coef = jnp.einsum("ics,irs->cr", leaf_coefs, leaf_transfer, precision=upper_level)
    coef_window = padded(leaf_coefs, (("leaf", 0),), leaf_count)
    far_valid = far_index >= 0
    far_local = jnp.where(far_valid, far_index - window_start, 0)
    picked = jnp.take(coef_window, far_local, axis=0) * far_valid[:, :, None, None].astype(
        jnp.float32
    )
    chosen = jnp.take(coupling_table, far_kind, axis=0)
    far_sum = jnp.einsum("ikcs,ikrs->icr", picked, chosen, precision=upper_level)
    depth_count = groups.bit_length() - 1
    ancestor = group_coef
    couplings = []
    for depth_step in range(depth_count):
        sibling = partner(ancestor, "leaf", depth_step)
        child_side = device_index >> depth_step & 1
        pair_number = (groups >> depth_step + 1) + (device_index >> depth_step + 1)
        kind_index = coarse_kind[pair_number - 1]
        coupling = coupling_table[kind_index]
        oriented = jnp.where(child_side == 0, coupling.T, coupling)
        couplings.append(jnp.dot(sibling, oriented, precision=upper_level))
        if depth_step + 1 < depth_count:
            ancestor = jnp.dot(
                ancestor, parent_transfer_matrices[child_side].T, precision=upper_level
            ) + jnp.dot(sibling, parent_transfer_matrices[1 - child_side].T, precision=upper_level)
    descending_pass = couplings[depth_count - 1]
    for depth_step in range(depth_count - 2, -1, -1):
        child_side = device_index >> depth_step & 1
        descending_pass = (
            jnp.dot(descending_pass, parent_transfer_matrices[child_side], precision=upper_level)
            + couplings[depth_step]
        )
    leaf_field = (
        jnp.einsum("cr,irs->ics", descending_pass, leaf_transfer, precision=upper_level) + far_sum
    )
    field_rounded = leaf_field.astype(jnp.bfloat16)
    far_rows = jnp.einsum(
        "ics,isq->ciq", field_rounded, cluster_basis, preferred_element_type=jnp.float32
    )
    vector_window = padded(vectors, (("leaf", 1),), vectors.shape[1])
    near_valid = near_index >= 0
    near_local = jnp.where(near_valid, near_index - window_start, 0)
    live_mask = near_valid.astype(jnp.bfloat16)
    blocks = lax.all_gather(near_blocks, "cols", axis=2, tiled=True)
    window_leaves = vector_window.reshape(cols_here, 3 * leaf_count, leaf_rows)
    picked_rows = jnp.take(window_leaves, near_local, axis=1) * live_mask[None, :, :, None]
    near_sum = jnp.einsum("cikr,ikqr->ciq", picked_rows, blocks, preferred_element_type=jnp.float32)
    summed = far_rows + near_sum
    return summed.reshape(cols_here, -1).astype(jnp.bfloat16)


def solution(mesh):
    in_specs = (
        P("cols", "leaf"),
        P("leaf", None, "cols", None),
        P("leaf", None),
        P("leaf", None),
        P("leaf", None),
        P("leaf", None, None),
        P("leaf", None, None),
        P(),
        P(),
        P(),
    )
    out_specs = P("cols", "leaf")
    return jax.shard_map(shards, mesh=mesh, in_specs=in_specs, out_specs=out_specs, check_vma=False)
```

profile of v0, /device:TPU:0, one launch (start us, length us, event | category | flops | bytes accessed | tf_op | source)
XLA Modules:
  0.0 79.1 jit_solution(911585325915295636)
XLA Ops:
  6.6 0.7 all-gather.2.cloned.1.call-update
  7.3 0.2 copy-done
  7.5 1.2 %fusion.28 = f32[8,64,64]{2,1,0:T(8,128)S(1)} fusion(bf16[8,64,256]{2,1,0:T(8,128)(2,1)S(1)} %copy-done, bf16[8,8,8,256]{3,2,1,0:T(8,128)(2,1)} %bitcast.30), kind=kOutput, calls=%fused_computation.37 | convolution fusion | flops 16777216 | bytes 655360 | tf_op jit(solution)/shard_map/cir,iqr->icq/dot_general | solution.py:50
  8.6 5.6 %collective-permute-start.4 = (f32[8,64,64]{2,1,0:T(8,128)S(1)}, f32[8,64,64]{2,1,0:T(8,128)}, u32[]{:S(2)}, u32[]{:S(2)}) collective-permute-start(f32[8,64,64]{2,1,0:T(8,128)S(1)} %fusion.28), channel_id=1, source_target_pairs={{0,2},{2,4},{4,6},{6,8},{8,10},{10,12},{12,14},{14,16},{16,18},{18... | collective-permute-start | bytes 393224 | tf_op jit(solution)/shard_map/ppermute | solution.py:14
  14.2 1.3 %collective-permute-start.5 = (f32[8,64,64]{2,1,0:T(8,128)S(1)}, f32[8,64,64]{2,1,0:T(8,128)}, u32[]{:S(2)}, u32[]{:S(2)}) collective-permute-start(f32[8,64,64]{2,1,0:T(8,128)S(1)} %fusion.28), channel_id=1, source_target_pairs={{2,0},{4,2},{6,4},{8,6},{10,8},{12,10},{14,12},{16,14},{18,16},{20... | collective-permute-start | bytes 393224 | tf_op jit(solution)/shard_map/ppermute | solution.py:15
  15.5 5.3 %collective-permute-start.6 = (bf16[64,2048]{1,0:T(8,128)(2,1)}, bf16[64,2048]{1,0:T(8,128)(2,1)}, u32[]{:S(2)}, u32[]{:S(2)}) collective-permute-start(bf16[64,2048]{1,0:T(8,128)(2,1)} %param.10), channel_id=1, source_target_pairs={{0,2},{2,4},{4,6},{6,8},{8,10},{10,12},{12,14},{14,16},{16,18},{18... | collective-permute-start | bytes 786440 | tf_op jit(solution)/shard_map/ppermute | solution.py:14
  20.8 1.3 %collective-permute-start.7 = (bf16[64,2048]{1,0:T(8,128)(2,1)}, bf16[64,2048]{1,0:T(8,128)(2,1)}, u32[]{:S(2)}, u32[]{:S(2)}) collective-permute-start(bf16[64,2048]{1,0:T(8,128)(2,1)} %param.10), channel_id=1, source_target_pairs={{2,0},{4,2},{6,4},{8,6},{10,8},{12,10},{14,12},{16,14},{18,16},{20... | collective-permute-start | bytes 786440 | tf_op jit(solution)/shard_map/ppermute | solution.py:15
  22.1 0.4 convolution_bitcast_fusion.1
  22.4 2.7 %collective-permute-start = (f32[64,64]{1,0:T(8,128)S(1)}, f32[64,64]{1,0:T(8,128)S(1)}, u32[]{:S(2)}, u32[]{:S(2)}) collective-permute-start(f32[64,64]{1,0:T(8,128)S(1)} %convolution_bitcast_fusion.1), channel_id=1, source_target_pairs={{0,2},{2,0},{4,6},{6,4},{8,10},{10,8},{12,14},{14,12},{16,18},{18,... | collective-permute-start | bytes 49160 | tf_op jit(solution)/shard_map/ppermute | solution.py:27
  25.1 0.7 fusion.73
  31.1 0.5 compare_and_fusion.2
  31.6 0.1 reshape.30
  31.7 0.1 reshape.38
  34.5 0.5 compare_and_fusion.1
  35.0 0.6 compare_and_fusion
  35.6 0.2 fusion.45
  35.8 0.1 reshape.46
  35.9 2.6 %collective-permute-done = f32[64,64]{1,0:T(8,128)S(1)} collective-permute-done((f32[64,64]{1,0:T(8,128)S(1)}, f32[64,64]{1,0:T(8,128)S(1)}, u32[]{:S(2)}, u32[]{:S(2)}) %collective-permute-start) | collective-permute-done | bytes 16416 | tf_op jit(solution)/shard_map/ppermute | solution.py:27
  38.5 0.2 convolution_add_fusion.6
  38.8 0.2 fusion.40
  39.0 3.7 %collective-permute-done.1 = f32[64,64]{1,0:T(8,128)S(1)} collective-permute-done((f32[64,64]{1,0:T(8,128)S(1)}, f32[64,64]{1,0:T(8,128)S(1)}, u32[]{:S(2)}, u32[]{:S(2)}) %collective-permute-start.1) | collective-permute-done | bytes 16416 | tf_op jit(solution)/shard_map/ppermute | solution.py:27
  42.7 0.2 convolution_add_fusion.5
  42.9 1.6 %collective-permute-start.2 = (f32[64,64]{1,0:T(8,128)S(1)}, f32[64,64]{1,0:T(8,128)S(1)}, u32[]{:S(2)}, u32[]{:S(2)}) collective-permute-start(f32[64,64]{1,0:T(8,128)S(1)} %convolution_add_fusion.5), channel_id=1, source_target_pairs={{0,8},{8,0},{2,10},{10,2},{4,12},{12,4},{6,14},{14,6},{16,24},{24,... | collective-permute-start | bytes 49160 | tf_op jit(solution)/shard_map/ppermute | solution.py:27
  44.6 0.2 fusion.35
  44.8 2.1 %collective-permute-done.2 = f32[64,64]{1,0:T(8,128)S(1)} collective-permute-done((f32[64,64]{1,0:T(8,128)S(1)}, f32[64,64]{1,0:T(8,128)S(1)}, u32[]{:S(2)}, u32[]{:S(2)}) %collective-permute-start.2) | collective-permute-done | bytes 16416 | tf_op jit(solution)/shard_map/ppermute | solution.py:27
  46.9 0.8 %convolution_add_fusion.4 = f32[64,64]{1,0:T(8,128)} fusion(f32[64,64]{1,0:T(8,128)S(1)} %fusion.35, f32[64,64]{1,0:T(8,128)S(1)} %collective-permute-done.2, f32[2,64,64]{2,1,0:T(8,128)S(1)} %copy-done.2, s32[]{:T(128)S(6)} %select_n.108), kind=kOutput, calls=%fused_computation.24 | convolution fusion | flops 3149824 | bytes 114692 | tf_op jit(solution)/shard_map/dot_general | solution.py:76
  47.7 2.6 %collective-permute-start.3 = (f32[64,64]{1,0:T(8,128)}, f32[64,64]{1,0:T(8,128)}, u32[]{:S(2)}, u32[]{:S(2)}) collective-permute-start(f32[64,64]{1,0:T(8,128)} %convolution_add_fusion.4), channel_id=1, source_target_pairs={{0,16},{16,0},{2,18},{18,2},{4,20},{20,4},{6,22},{22,6},{8,24},{24... | collective-permute-start | bytes 49160 | tf_op jit(solution)/shard_map/ppermute | solution.py:27
  50.3 0.7 copy.24
  51.1 0.1 copy.26
  51.2 0.7 gather_fusion.1
  51.9 0.9 %collective-permute-done.3 = f32[64,64]{1,0:T(8,128)} collective-permute-done((f32[64,64]{1,0:T(8,128)}, f32[64,64]{1,0:T(8,128)}, u32[]{:S(2)}, u32[]{:S(2)}) %collective-permute-start.3) | collective-permute-done | bytes 16416 | tf_op jit(solution)/shard_map/ppermute | solution.py:27
  52.8 0.9 %fusion.31 = f32[64,64]{1,0:T(8,128)S(1)} fusion(f32[64,64]{1,0:T(8,128)} %collective-permute-done.3, f32[64,64]{1,0:T(8,128)S(1)} %get-tuple-element.12, f32[64,64]{0,1:T(8,128)} %copy.24, pred[]{:T(512)S(6)} %eq.12), kind=kOutput, calls=%fused_computation.44 | convolution fusion | flops 3149824 | bytes 65537 | tf_op jit(solution)/shard_map/dot_general | solution.py:72
  53.8 0.2 fusion.33
  54.0 0.9 %convolution_add_fusion.3 = f32[64,64]{1,0:T(8,128)S(1)} fusion(f32[64,64]{1,0:T(8,128)S(1)} %fusion.33, f32[64,64]{1,0:T(8,128)} %copy-done.5, f32[64,64]{1,0:T(8,128)S(1)} %get-tuple-element.11, f32[64,64]{0,1:T(8,128)S(1)} %copy.25, pred[]{:T(512)S(6)} %eq.13), kind=kOutput, calls=%fused_computation.23 | convolution fusion | flops 3153920 | bytes 81921 | tf_op jit(solution)/shard_map/dot_general | solution.py:72
  54.9 0.2 fusion.38
  55.1 0.2 convolution_add_fusion.2
  55.2 0.2 fusion.43
  55.4 0.2 fusion.21
  55.6 1.1 %pad_maximum_fusion = f32[24,64,64]{2,1,0:T(8,128)S(1)} fusion(f32[8,64,64]{2,1,0:T(8,128)} %collective-permute-done.5, f32[8,64,64]{2,1,0:T(8,128)S(1)} %fusion.28, f32[8,64,64]{2,1,0:T(8,128)} %collective-permute-done.4), kind=kLoop, calls=%fused_computation.35 | loop fusion | flops 196608 | bytes 786432 | tf_op jit(solution)/shard_map/concatenate | solution.py:16
  56.7 2.1 %gather_fusion = f32[64,64,64]{2,1,0:T(8,128)} fusion(f32[24,64,64]{2,1,0:T(8,128)S(1)} %pad_maximum_fusion, s32[1024]{0:T(1024)S(1)} %pad_clamp_fusion.2), kind=kCustom, calls=%fused_computation | custom fusion | bytes 2097408 | tf_op jit(solution)/shard_map/jit(_take)/gather | solution.py:57
  58.8 4.1 %fusion.15 = f32[8,64,64]{2,1,0:T(8,128)S(1)} fusion(f32[8,8,64,64]{3,2,1,0:T(8,128)S(1)} %bitcast.106, f32[8,8,64,64]{3,2,1,0:T(8,128)} %bitcast.107, f32[8,8]{1,0:T(8,128)S(1)} %get-tuple-element.13, pred[8,8]{1,0:T(8,128)(4,1)S(1)} %copy-done.9, pred[8,8]{1,0:T(8,128)(4,1)S(1)} %copy-done.8), kind=kOutput, calls=%fused_computation.18 | convolution fusion | flops 202113024 | bytes 2228608 | tf_op jit(solution)/shard_map/ikcs,ikrs->icr/dot_general | solution.py:61
  62.9 0.4 fusion.20
  63.3 1.2 %pad_maximum_fusion.1 = bf16[64,6144]{1,0:T(8,128)(2,1)S(1)} fusion(bf16[64,2048]{1,0:T(8,128)(2,1)} %collective-permute-done.7, bf16[64,2048]{1,0:T(8,128)(2,1)} %param.10, bf16[64,2048]{1,0:T(8,128)(2,1)} %collective-permute-done.6), kind=kLoop, calls=%fused_computation.36 | loop fusion | flops 2359296 | bytes 1572864 | tf_op jit(solution)/shard_map/concatenate | solution.py:16
  64.4 0.1 copy.40
  64.6 0.7 gather_fusion.2
  65.3 6.0 %fusion.9 = f32[8,64,256]{2,1,0:T(8,128)S(1)} fusion(bf16[8,8,256,256]{3,2,1,0:T(8,128)(2,1)} %all-gather.2.cloned.1.call-done, bf16[8,8,64,256]{3,2,1,0:T(8,128)(2,1)S(1)} %bitcast.109, pred[8,8]{1,0:T(8,128)(4,1)S(1)} %copy-done.13, bf16[8,8]{1,0:T(8,128)(2,1)S(1)} %copy-done.12), kind=kOutput, calls=%fused_computation.13 | convolution fusion | flops 538968064 | bytes 11010240 | tf_op jit(solution)/shard_map/cikr,ikqr->ciq/dot_general | solution.py:98
  71.3 0.2 fusion.13
  71.5 0.7 copy.34
  (41 shorter events, 0.4 us)
Async XLA Ops:
  6.5 1.0 %copy-start = (bf16[8,64,256]{2,1,0:T(8,128)(2,1)S(1)}, bf16[8,64,256]{2,1,0:T(8,128)(2,1)}, u32[]{:S(2)}) copy-start(bf16[8,64,256]{2,1,0:T(8,128)(2,1)} %param.15) | copy-start | bytes 786436
  6.5 15.5 %copy-start.3 = (f32[8,64,64]{2,1,0:T(8,128)S(1)}, f32[8,64,64]{2,1,0:T(8,128)}, u32[]{:S(2)}) copy-start(f32[8,64,64]{2,1,0:T(8,128)} %param.16) | copy-start | bytes 393220
  6.5 18.6 %copy-start.7 = (s32[15]{0:T(128)S(1)}, s32[15]{0:T(128)}, u32[]{:S(2)}) copy-start(s32[15]{0:T(128)} %param.19) | copy-start | bytes 184
  6.5 24.5 %copy-start.10 = (s32[8,8]{1,0:T(8,128)S(1)}, s32[8,8]{1,0:T(8,128)}, u32[]{:S(2)}) copy-start(s32[8,8]{1,0:T(8,128)} %param.13) | copy-start | bytes 772
  6.5 25.2 %copy-start.6 = (s32[8,8]{1,0:T(8,128)S(1)}, s32[8,8]{1,0:T(8,128)}, u32[]{:S(2)}) copy-start(s32[8,8]{1,0:T(8,128)} %param.14) | copy-start | bytes 772
  6.5 27.9 %copy-start.1 = (f32[16,64,64]{2,1,0:T(8,128)S(1)}, f32[16,64,64]{2,1,0:T(8,128)}, u32[]{:S(2)}) copy-start(f32[16,64,64]{2,1,0:T(8,128)} %param.17) | copy-start | bytes 786436
  6.6 28.5 %copy-start.11 = (s32[8,8]{1,0:T(8,128)S(1)}, s32[8,8]{1,0:T(8,128)}, u32[]{:S(2)}) copy-start(s32[8,8]{1,0:T(8,128)} %param.12) | copy-start | bytes 772
  6.6 29.1 %copy-start.2 = (f32[2,64,64]{2,1,0:T(8,128)S(1)}, f32[2,64,64]{2,1,0:T(8,128)}, u32[]{:S(2)}) copy-start(f32[2,64,64]{2,1,0:T(8,128)} %param.18) | copy-start | bytes 98308
  6.6 58.7 %all-gather.2.cloned.1.call-start = ((), (), s32[]{:S(2)}) async-start(), calls=%async_computation | async-start | bytes 12582912 | tf_op jit(solution)/shard_map/all_gather | solution.py:95
  8.6 46.9 %collective-permute-start.4 = (f32[8,64,64]{2,1,0:T(8,128)S(1)}, f32[8,64,64]{2,1,0:T(8,128)}, u32[]{:S(2)}, u32[]{:S(2)}) collective-permute-start(f32[8,64,64]{2,1,0:T(8,128)S(1)} %fusion.28), channel_id=1, source_target_pairs={{0,2},{2,4},{4,6},{6,8},{8,10},{10,12},{12,14},{14,16},{16,18},{18... | collective-permute-start | bytes 393224 | tf_op jit(solution)/shard_map/ppermute | solution.py:14
  14.2 41.4 %collective-permute-start.5 = (f32[8,64,64]{2,1,0:T(8,128)S(1)}, f32[8,64,64]{2,1,0:T(8,128)}, u32[]{:S(2)}, u32[]{:S(2)}) collective-permute-start(f32[8,64,64]{2,1,0:T(8,128)S(1)} %fusion.28), channel_id=1, source_target_pairs={{2,0},{4,2},{6,4},{8,6},{10,8},{12,10},{14,12},{16,14},{18,16},{20... | collective-permute-start | bytes 393224 | tf_op jit(solution)/shard_map/ppermute | solution.py:15
  15.5 47.8 %collective-permute-start.6 = (bf16[64,2048]{1,0:T(8,128)(2,1)}, bf16[64,2048]{1,0:T(8,128)(2,1)}, u32[]{:S(2)}, u32[]{:S(2)}) collective-permute-start(bf16[64,2048]{1,0:T(8,128)(2,1)} %param.10), channel_id=1, source_target_pairs={{0,2},{2,4},{4,6},{6,8},{8,10},{10,12},{12,14},{14,16},{16,18},{18... | collective-permute-start | bytes 786440 | tf_op jit(solution)/shard_map/ppermute | solution.py:14
  20.8 42.5 %collective-permute-start.7 = (bf16[64,2048]{1,0:T(8,128)(2,1)}, bf16[64,2048]{1,0:T(8,128)(2,1)}, u32[]{:S(2)}, u32[]{:S(2)}) collective-permute-start(bf16[64,2048]{1,0:T(8,128)(2,1)} %param.10), channel_id=1, source_target_pairs={{2,0},{4,2},{6,4},{8,6},{10,8},{12,10},{14,12},{16,14},{18,16},{20... | collective-permute-start | bytes 786440 | tf_op jit(solution)/shard_map/ppermute | solution.py:15
  22.4 16.1 %collective-permute-start = (f32[64,64]{1,0:T(8,128)S(1)}, f32[64,64]{1,0:T(8,128)S(1)}, u32[]{:S(2)}, u32[]{:S(2)}) collective-permute-start(f32[64,64]{1,0:T(8,128)S(1)} %convolution_bitcast_fusion.1), channel_id=1, source_target_pairs={{0,2},{2,0},{4,6},{6,4},{8,10},{10,8},{12,14},{14,12},{16,18},{18,... | collective-permute-start | bytes 49160 | tf_op jit(solution)/shard_map/ppermute | solution.py:27
  38.7 4.0 %collective-permute-start.1 = (f32[64,64]{1,0:T(8,128)S(1)}, f32[64,64]{1,0:T(8,128)S(1)}, u32[]{:S(2)}, u32[]{:S(2)}) collective-permute-start(f32[64,64]{1,0:T(8,128)S(1)} %convolution_add_fusion.6), channel_id=1, source_target_pairs={{0,4},{4,0},{2,6},{6,2},{8,12},{12,8},{10,14},{14,10},{16,20},{20,... | collective-permute-start | bytes 49160 | tf_op jit(solution)/shard_map/ppermute | solution.py:27
  42.9 4.0 %collective-permute-start.2 = (f32[64,64]{1,0:T(8,128)S(1)}, f32[64,64]{1,0:T(8,128)S(1)}, u32[]{:S(2)}, u32[]{:S(2)}) collective-permute-start(f32[64,64]{1,0:T(8,128)S(1)} %convolution_add_fusion.5), channel_id=1, source_target_pairs={{0,8},{8,0},{2,10},{10,2},{4,12},{12,4},{6,14},{14,6},{16,24},{24,... | collective-permute-start | bytes 49160 | tf_op jit(solution)/shard_map/ppermute | solution.py:27
  46.9 4.3 %copy-start.5 = (f32[64,64]{1,0:T(8,128)}, f32[64,64]{1,0:T(8,128)S(1)}, u32[]{:S(2)}) copy-start(f32[64,64]{1,0:T(8,128)S(1)} %collective-permute-done.2) | copy-start | bytes 49156
  47.7 5.1 %collective-permute-start.3 = (f32[64,64]{1,0:T(8,128)}, f32[64,64]{1,0:T(8,128)}, u32[]{:S(2)}, u32[]{:S(2)}) collective-permute-start(f32[64,64]{1,0:T(8,128)} %convolution_add_fusion.4), channel_id=1, source_target_pairs={{0,16},{16,0},{2,18},{18,2},{4,20},{20,4},{6,22},{22,6},{8,24},{24... | collective-permute-start | bytes 49160 | tf_op jit(solution)/shard_map/ppermute | solution.py:27
  56.7 2.1 %copy-start.8 = (pred[8,8]{1,0:T(8,128)(4,1)S(1)}, pred[8,8]{1,0:T(8,128)(4,1)}, u32[]{:S(2)}) copy-start(pred[8,8]{1,0:T(8,128)(4,1)} %get-tuple-element.5) | copy-start | bytes 196
  56.7 2.1 %copy-start.9 = (pred[8,8]{1,0:T(8,128)(4,1)S(1)}, pred[8,8]{1,0:T(8,128)(4,1)}, u32[]{:S(2)}) copy-start(pred[8,8]{1,0:T(8,128)(4,1)} %compare_and_fusion.1) | copy-start | bytes 196
  58.8 4.1 %copy-start.4 = (f32[8,64,64]{2,1,0:T(8,128)S(1)}, f32[8,64,64]{2,1,0:T(8,128)}, u32[]{:S(2)}) copy-start(f32[8,64,64]{2,1,0:T(8,128)} %param.16) | copy-start | bytes 393220
  64.5 0.7 copy-start.12
  64.5 0.7 copy-start.13
Sparse Core Ops, SparseCore 0:
  9.0 22.5 all-gather.1
where the time goes:
time: 79.7 us; the launch traced here: 79.1 us
  between operations  21.7 us (27%)
  starting transfers between devices  20.4 us (26%)
  matrix products  16.6 us (21%)
  waiting for transfers between devices  10.1 us (13%)
  local copies, waits for them, and re-layouts  6.32 us (8%)
  other arithmetic  3.94 us (5%)
    ppermute x2, starting transfers between devices, padded(): before = lax.ppermute(last, axis, up)  10.8 us
    ppermute x4, waiting for transfers between devices, partner(): return lax.ppermute(block, axis, route)  9.37 us
    ppermute x4, starting transfers between devices, partner(): return lax.ppermute(block, axis, route)  7.01 us
    dot_general x1, matrix products, shards(): jnp.einsum('cikr,ikqr->ciq', picked_rows, blocks, preferred_element_type=...  6.03 us
    dot_general x1, matrix products, shards(): jnp.einsum('ikcs,ikrs->icr', picked, chosen, precision=upper_level)  4.07 us
    ppermute x2, starting transfers between devices, padded(): after = lax.ppermute(leading, axis, down)  2.56 us
    concatenate x2, other arithmetic, padded(): array = jnp.concatenate([before, array, after], axis=dim)  2.26 us
    dot_general x4, matrix products, shards(): couplings.append(jnp.dot(sibling, oriented, precision=upper_level))  2.19 us
  transfers between devices with their start and end apart: 9, of which 4 were waited for; matrix products, arithmetic and copies ran while one was open for 25% of the time, Pallas kernels for 0%

commit v1 on v0

v1 whole, which is shorter than its diff:
```python
import functools

import jax
import jax.numpy as jnp
from jax import lax
from jax.experimental import pallas as pl
from jax.experimental.pallas import tpu as pltpu
from jax.sharding import PartitionSpec as P

HI = lax.Precision.HIGHEST
F32 = jnp.float32
BF16 = jnp.bfloat16
CHUNKS = 2


def nt(a, b, precision=None):
    return lax.dot_general(
        a, b, (((1,), (1,)), ((), ())), precision=precision, preferred_element_type=F32
    )


def nn(a, b, precision=None):
    return jnp.dot(a, b, precision=precision, preferred_element_type=F32)


def kernel(
    n, x_ref, near_hbm, near_idx, far_idx, far_kind, basis, transfer, table, parents, kinds,
    out, xw, cw, blocks, up_out, up_in, near_out, near_in, total, own_near, table16,
    send, recv, local,
):
    me, core = lax.axis_index("leaf"), lax.axis_index("cols")
    other = 1 - core
    leaves, slots = near_idx.shape
    far_slots = far_idx.shape[1]
    rows = basis.shape[2]
    half = near_hbm.shape[2]
    cols = x_ref.shape[0]
    depth = n.bit_length() - 1
    side = lax.rem(me, 2)
    pair = me + 1 - 2 * side
    onward, source = me + 2 - 4 * side, me - 2 + 4 * side
    has_onward = jnp.logical_and(onward >= 0, onward < n)
    has_source = jnp.logical_and(source >= 0, source < n)
    there = side * 2 * leaves
    direct = (1 - side) * 2 * leaves
    relayed = side * 2 * leaves
    part = leaves // CHUNKS
    mirror = lambda l: me + (1 - 2 * (lax.rem(me // (1 << l), 2))) * (1 << l)

    barrier = pltpu.get_barrier_semaphore()

    def greet(leaf, c):
        pl.semaphore_signal(
            barrier, inc=1, device_id=(leaf, c), device_id_type=pl.DeviceIdType.MESH
        )

    greet(me, other)
    greet(pair, core)
    for level in range(2, depth):
        greet(mirror(level), core)

    @pl.when(has_onward)
    def _():
        greet(onward, core)

    @pl.when(has_source)
    def _():
        greet(source, core)

    def fetch(i):
        return pltpu.make_async_copy(near_hbm.at[i], blocks.at[i], local.at[i])

    for i in range(leaves):
        fetch(i).start()
    for i in range(leaves):
        xw[core, leaves + i] = x_ref[:, i * rows : (i + 1) * rows]

    @pl.when(jnp.logical_not(has_source))
    def _():
        xw[0, pl.ds(relayed, leaves)] = jnp.zeros((leaves, cols, rows), BF16)
        xw[1, pl.ds(relayed, leaves)] = jnp.zeros((leaves, cols, rows), BF16)
        cw[pl.ds(relayed, leaves)] = jnp.zeros((leaves,) + cw.shape[1:], BF16)

    peers = depth + has_onward.astype(jnp.int32) + has_source.astype(jnp.int32)
    pl.semaphore_wait(barrier, peers)

    def copy(src, dst, s, leaf, c):
        return pltpu.make_async_remote_copy(
            src_ref=src, dst_ref=dst, send_sem=send.at[s], recv_sem=recv.at[s],
            device_id=(leaf, c), device_id_type=pl.DeviceIdType.MESH,
        )

    def at(c, start, h):
        return xw.at[c, pl.ds(start + h * part, part)]

    def to_pair(h):
        return copy(at(core, leaves, h), at(core, there, h), h, pair, core)

    def from_pair(h):
        return copy(at(core, direct, h), at(core, direct, h), h, pair, core)

    def relay(h):
        return copy(at(core, direct, h), at(core, there, h), CHUNKS + h, onward, core)

    def from_relay(h):
        return copy(at(core, relayed, h), at(core, relayed, h), CHUNKS + h, source, core)

    def across(which, start, h):
        return copy(
            at(core, start, h), at(core, start, h), (2 + which) * CHUNKS + h, me, other
        )

    def from_across(which, start, h):
        return copy(
            at(other, start, h), at(other, start, h), (2 + which) * CHUNKS + h, me, other
        )

    base = 5 * CHUNKS
    own_cw = cw.at[pl.ds(leaves, leaves)]
    direct_cw = cw.at[pl.ds(direct, leaves)]
    relayed_cw = cw.at[pl.ds(relayed, leaves)]
    there_cw = cw.at[pl.ds(there, leaves)]
    coef_pair = copy(own_cw, there_cw, base, pair, core)
    coef_from_pair = copy(direct_cw, direct_cw, base, pair, core)
    coef_relay = copy(direct_cw, there_cw, base + 1, onward, core)
    coef_from_relay = copy(relayed_cw, relayed_cw, base + 1, source, core)

    def up(level):
        return copy(up_out.at[level], up_in.at[level], base + 2 + level, mirror(level), core)

    def near_copy(i):
        return copy(near_out.at[i], near_in.at[i], base + 2 + depth + i, me, other)

    for h in range(CHUNKS):
        to_pair(h).start()
    for h in range(CHUNKS):
        across(0, leaves, h).start()

    ancestor = jnp.zeros((cols, basis.shape[1]), F32)
    for i in range(leaves):
        coef = nt(x_ref[:, i * rows : (i + 1) * rows], basis[i])
        cw[leaves + i] = coef.astype(BF16)
        ancestor += nt(coef, transfer[i], HI)
    up_out[0] = ancestor
    up(0).start()
    coef_pair.start()
    table16[...] = table[...].astype(BF16)

    def hand_on(h):
        from_pair(h).wait_recv()

        @pl.when(has_onward)
        def _():
            relay(h).start()

        across(1, direct, h).start()

    def pass_across(h):
        @pl.when(has_source)
        def _():
            from_relay(h).wait_recv()
            across(2, relayed, h).start()

    def hand_coefs_on():
        coef_from_pair.wait_recv()

        @pl.when(has_onward)
        def _():
            coef_relay.start()

    def coefs_in():
        @pl.when(has_source)
        def _():
            coef_from_relay.wait_recv()

    tasks = [functools.partial(hand_on, h) for h in range(CHUNKS)]
    tasks.insert(1, hand_coefs_on)
    tasks += [functools.partial(pass_across, h) for h in range(CHUNKS)]
    tasks.insert(4, coefs_in)

    couplings = []
    for level in range(depth):
        up(level).wait_recv()
        sibling = up_in[level]
        child = lax.rem(me // (1 << level), 2)
        if level + 1 < depth:
            ancestor = nt(ancestor, parents[child], HI) + nt(sibling, parents[1 - child], HI)
            up_out[level + 1] = ancestor
            up(level + 1).start()
        if tasks:
            tasks.pop(0)()
        number = (n // (2 << level)) + me // (2 << level)
        coupling = table[kinds[number - 1]]
        couplings.append(
            jnp.where(child == 0, nt(sibling, coupling, HI), nn(sibling, coupling, HI))
        )
    down = couplings[depth - 1]
    for level in range(depth - 2, -1, -1):
        child = lax.rem(me // (1 << level), 2)
        down = nn(down, parents[child], HI) + couplings[level]
    for task in tasks:
        task()
    first = (me - 1) * leaves

    def window(index):
        inside = jnp.minimum(jnp.maximum(index - first, 0), 3 * leaves - 1)
        return jnp.where(index >= 0, inside, leaves)

    def far(i, carry):
        field = nn(down, transfer[i], HI)
        for k in range(far_slots):
            index = far_idx[i, k]
            live = index >= 0
            picked = cw[window(index)]
            picked = jnp.where(live, picked, jnp.zeros_like(picked))
            field += nt(picked, table16[far_kind[i, k]])
        total[i] = nn(field.astype(BF16), basis[i])
        return carry

    lax.fori_loop(0, leaves, far, 0)

    for h in range(CHUNKS):
        from_across(0, leaves, h).wait_recv()
        from_across(1, direct, h).wait_recv()

    @pl.when(has_source)
    def _():
        for h in range(CHUNKS):
            from_across(2, relayed, h).wait_recv()

    for i in range(leaves):
        fetch(i).wait()

    def near(i, carry):
        mine = jnp.zeros((cols, half), F32)
        theirs = jnp.zeros((cols, half), F32)
        for k in range(slots):
            index = near_idx[i, k]
            live = index >= 0
            place = window(index)
            picked = jnp.concatenate([xw[core, place], xw[other, place]], axis=0)
            picked = jnp.where(live, picked, jnp.zeros_like(picked))
            both = nt(picked, blocks[i, k])
            mine += both[:cols]
            theirs += both[cols:]
        near_out[i] = theirs
        near_copy(i).start()
        own_near[i] = mine
        return carry

    lax.fori_loop(0, leaves, near, 0)

    here = pl.multiple_of(core * half, half)
    across_half = pl.multiple_of(other * half, half)
    for i in range(leaves):
        out[:, pl.ds(i * rows + here, half)] = (
            total[i, :, pl.ds(here, half)] + own_near[i]
        ).astype(BF16)
    for i in range(leaves):
        near_copy(i).wait_recv()
        out[:, pl.ds(i * rows + across_half, half)] = (
            total[i, :, pl.ds(across_half, half)] + near_in[i]
        ).astype(BF16)

    for h in range(CHUNKS):
        to_pair(h).wait_send()
        across(0, leaves, h).wait_send()
        across(1, direct, h).wait_send()
    coef_pair.wait_send()
    for level in range(depth):
        up(level).wait_send()
    for i in range(leaves):
        near_copy(i).wait_send()

    @pl.when(has_onward)
    def _():
        for h in range(CHUNKS):
            relay(h).wait_send()
        coef_relay.wait_send()

    @pl.when(has_source)
    def _():
        for h in range(CHUNKS):
            across(2, relayed, h).wait_send()


def shards(
    vectors, near_blocks, near_index, far_index, far_kind, cluster_basis, leaf_transfer,
    coupling_table, parent_transfer_matrices, coarse_kind,
):
    n = lax.axis_size("leaf")
    depth = n.bit_length() - 1
    cols = vectors.shape[0]
    leaves, rank, rows = cluster_basis.shape
    half = near_blocks.shape[2]
    copies = 5 * CHUNKS + 2 + depth + leaves
    vmem = pl.BlockSpec(memory_space=pltpu.VMEM)
    smem = pl.BlockSpec(memory_space=pltpu.SMEM)
    hbm = pl.BlockSpec(memory_space=pl.ANY)
    return pl.pallas_call(
        functools.partial(kernel, n),
        out_shape=jax.ShapeDtypeStruct(vectors.shape, BF16),
        in_specs=[vmem, hbm, smem, smem, smem, vmem, vmem, vmem, vmem, smem],
        out_specs=vmem,
        scratch_shapes=[
            pltpu.VMEM((2, 3 * leaves, cols, rows), BF16),
            pltpu.VMEM((3 * leaves, cols, rank), BF16),
            pltpu.VMEM(near_blocks.shape, BF16),
            pltpu.VMEM((depth, cols, rank), F32),
            pltpu.VMEM((depth, cols, rank), F32),
            pltpu.VMEM((leaves, cols, half), F32),
            pltpu.VMEM((leaves, cols, half), F32),
            pltpu.VMEM((leaves, cols, rows), F32),
            pltpu.VMEM((leaves, cols, half), F32),
            pltpu.VMEM(coupling_table.shape, BF16),
            pltpu.SemaphoreType.DMA((copies,)),
            pltpu.SemaphoreType.DMA((copies,)),
            pltpu.SemaphoreType.DMA((leaves,)),
        ],
        compiler_params=pltpu.CompilerParams(
            collective_id=0, has_side_effects=True, vmem_limit_bytes=40 << 20
        ),
        cost_estimate=pl.CostEstimate(flops=10**9, bytes_accessed=6 << 20, transcendentals=0),
    )(
        vectors, near_blocks, near_index, far_index, far_kind, cluster_basis, leaf_transfer,
        coupling_table, parent_transfer_matrices, coarse_kind,
    )


def solution(mesh):
    in_specs = (
        P("cols", "leaf"),
        P("leaf", None, "cols", None),
        P("leaf", None),
        P("leaf", None),
        P("leaf", None),
        P("leaf", None, None),
        P("leaf", None, None),
        P(),
        P(),
        P(),
    )
    out_specs = P("cols", "leaf")
    return jax.shard_map(shards, mesh=mesh, in_specs=in_specs, out_specs=out_specs, check_vma=False)
```

time: 79.7 us -> 44.4 us (0.56)
  the two profiles are of different devices: /device:TPU:0 before, /device:TPU:5 now
where the time goes in v1:
time: 44.4 us; the launch traced here: 44 us
  Pallas kernels  33.6 us (76%)
  local copies, waits for them, and re-layouts  10.3 us (23%)
    pallas_call x1, Pallas kernels, shards(): pl.pallas_call(functools.partial(kernel, n), out_shape=jax.ShapeDtypeStru...  33.6 us
    unnamed x21, local copies, waits for them, and re-layouts  10.3 us

profile of v1, /device:TPU:5, one launch (start us, length us, event | category | flops | bytes accessed | tf_op | source)
XLA Modules:
  0.0 44.0 jit_solution(11715499954539569081)
XLA Ops:
  0.0 0.0 copy-start
  0.0 2.2 %copy-done = bf16[8,8,128,256]{3,2,1,0:T(8,128)(2,1)S(1)} copy-done((bf16[8,8,128,256]{3,2,1,0:T(8,128)(2,1)S(1)}, bf16[8,8,128,256]{3,2,1,0:T(8,128)(2,1)}, u32[]{:S(2)}) %copy-start) | copy-done | bytes 4194328
  2.2 0.0 copy-start.1
  2.2 1.0 %copy-done.1 = f32[16,64,64]{2,1,0:T(8,128)S(1)} copy-done((f32[16,64,64]{2,1,0:T(8,128)S(1)}, f32[16,64,64]{2,1,0:T(8,128)}, u32[]{:S(2)}) %copy-start.1) | copy-done | bytes 262168
  3.2 0.0 copy-start.2
  3.2 0.9 %copy-done.2 = bf16[64,2048]{1,0:T(8,128)(2,1)S(1)} copy-done((bf16[64,2048]{1,0:T(8,128)(2,1)S(1)}, bf16[64,2048]{1,0:T(8,128)(2,1)}, u32[]{:S(2)}) %copy-start.2) | copy-done | bytes 262168
  4.2 0.0 copy-start.3
  4.2 0.9 %copy-done.3 = bf16[8,64,256]{2,1,0:T(8,128)(2,1)S(1)} copy-done((bf16[8,64,256]{2,1,0:T(8,128)(2,1)S(1)}, bf16[8,64,256]{2,1,0:T(8,128)(2,1)}, u32[]{:S(2)}) %copy-start.3) | copy-done | bytes 262168
  5.1 0.0 copy-start.4
  5.1 0.9 %copy-done.4 = f32[8,64,64]{2,1,0:T(8,128)S(1)} copy-done((f32[8,64,64]{2,1,0:T(8,128)S(1)}, f32[8,64,64]{2,1,0:T(8,128)}, u32[]{:S(2)}) %copy-start.4) | copy-done | bytes 131096
  6.1 0.0 copy-start.5
  6.1 0.8 %copy-done.5 = f32[2,64,64]{2,1,0:T(8,128)S(1)} copy-done((f32[2,64,64]{2,1,0:T(8,128)S(1)}, f32[2,64,64]{2,1,0:T(8,128)}, u32[]{:S(2)}) %copy-start.5) | copy-done | bytes 32792
  6.9 0.0 copy-start.6
  6.9 0.7 %copy-done.6 = s32[8,8]{1,0:T(8,128)S(1)} copy-done((s32[8,8]{1,0:T(8,128)S(1)}, s32[8,8]{1,0:T(8,128)}, u32[]{:S(2)}) %copy-start.6) | copy-done | bytes 280
  7.6 0.0 copy-start.7
  7.6 0.7 %copy-done.7 = s32[8,8]{1,0:T(8,128)S(1)} copy-done((s32[8,8]{1,0:T(8,128)S(1)}, s32[8,8]{1,0:T(8,128)}, u32[]{:S(2)}) %copy-start.7) | copy-done | bytes 280
  8.3 0.0 copy-start.8
  8.3 0.7 %copy-done.8 = s32[8,8]{1,0:T(8,128)S(1)} copy-done((s32[8,8]{1,0:T(8,128)S(1)}, s32[8,8]{1,0:T(8,128)}, u32[]{:S(2)}) %copy-start.8) | copy-done | bytes 280
  9.0 0.0 copy-start.9
  9.0 0.7 %copy-done.9 = s32[15]{0:T(128)S(1)} copy-done((s32[15]{0:T(128)S(1)}, s32[15]{0:T(128)}, u32[]{:S(2)}) %copy-start.9) | copy-done | bytes 84
  9.6 33.6 %shard_map.100 = bf16[64,2048]{1,0:T(8,128)(2,1)S(1)} custom-call(bf16[64,2048]{1,0:T(8,128)(2,1)S(1)} %copy-done.2, bf16[8,8,128,256]{3,2,1,0:T(8,128)(2,1)S(1)} %copy-done, s32[8,8]{1,0:T(8,128)S(1)} %copy-done.6, s32[8,8]{1,0:T(8,128)S(1)} %copy-done.7, s32[8,8]{1,0:T(8,128)S(1)} %copy-done.8, bf16[8,64,256]{2,1,0:T(8,128)(2,1)S(1)} %copy-done.3, ...), custom_call_target="tpu_custom_call" | custom-call | flops 1000000000 | bytes 6291456 | tf_op jit(solution)/shard_map/pallas_call | solution.py:300
  43.3 0.7 %copy.12 = bf16[64,2048]{1,0:T(8,128)(2,1)} copy(bf16[64,2048]{1,0:T(8,128)(2,1)S(1)} %shard_map.100) | data formatting | bytes 524288
Async XLA Ops:
  0.0 2.2 %copy-start = (bf16[8,8,128,256]{3,2,1,0:T(8,128)(2,1)S(1)}, bf16[8,8,128,256]{3,2,1,0:T(8,128)(2,1)}, u32[]{:S(2)}) copy-start(bf16[8,8,128,256]{3,2,1,0:T(8,128)(2,1)} %near_hbm.1) | copy-start | bytes 12582916
  2.2 1.0 %copy-start.1 = (f32[16,64,64]{2,1,0:T(8,128)S(1)}, f32[16,64,64]{2,1,0:T(8,128)}, u32[]{:S(2)}) copy-start(f32[16,64,64]{2,1,0:T(8,128)} %table.1) | copy-start | bytes 786436
  3.2 0.9 %copy-start.2 = (bf16[64,2048]{1,0:T(8,128)(2,1)S(1)}, bf16[64,2048]{1,0:T(8,128)(2,1)}, u32[]{:S(2)}) copy-start(bf16[64,2048]{1,0:T(8,128)(2,1)} %x_ref.1) | copy-start | bytes 786436
  4.2 0.9 %copy-start.3 = (bf16[8,64,256]{2,1,0:T(8,128)(2,1)S(1)}, bf16[8,64,256]{2,1,0:T(8,128)(2,1)}, u32[]{:S(2)}) copy-start(bf16[8,64,256]{2,1,0:T(8,128)(2,1)} %basis.1) | copy-start | bytes 786436
  5.1 0.9 %copy-start.4 = (f32[8,64,64]{2,1,0:T(8,128)S(1)}, f32[8,64,64]{2,1,0:T(8,128)}, u32[]{:S(2)}) copy-start(f32[8,64,64]{2,1,0:T(8,128)} %transfer.1) | copy-start | bytes 393220
  6.1 0.8 %copy-start.5 = (f32[2,64,64]{2,1,0:T(8,128)S(1)}, f32[2,64,64]{2,1,0:T(8,128)}, u32[]{:S(2)}) copy-start(f32[2,64,64]{2,1,0:T(8,128)} %parents.1) | copy-start | bytes 98308
  6.9 0.7 %copy-start.6 = (s32[8,8]{1,0:T(8,128)S(1)}, s32[8,8]{1,0:T(8,128)}, u32[]{:S(2)}) copy-start(s32[8,8]{1,0:T(8,128)} %near_idx.1) | copy-start | bytes 772
  7.6 0.7 %copy-start.7 = (s32[8,8]{1,0:T(8,128)S(1)}, s32[8,8]{1,0:T(8,128)}, u32[]{:S(2)}) copy-start(s32[8,8]{1,0:T(8,128)} %far_idx.1) | copy-start | bytes 772
  8.3 0.7 %copy-start.8 = (s32[8,8]{1,0:T(8,128)S(1)}, s32[8,8]{1,0:T(8,128)}, u32[]{:S(2)}) copy-start(s32[8,8]{1,0:T(8,128)} %far_kind.1) | copy-start | bytes 772
  9.0 0.7 %copy-start.9 = (s32[15]{0:T(128)S(1)}, s32[15]{0:T(128)}, u32[]{:S(2)}) copy-start(s32[15]{0:T(128)} %kinds.1) | copy-start | bytes 184

commit v2 on v1

--- a/solution.py
+++ b/solution.py
@@ -24,9 +24,11 @@
 
 
 def kernel(
-    n, x_ref, near_hbm, near_idx, far_idx, far_kind, basis, transfer, table, parents, kinds,
-    out, xw, cw, blocks, up_out, up_in, near_out, near_in, total, own_near, table16,
-    send, recv, local,
+    n, x_hbm, near_hbm, near_idx_hbm, far_idx_hbm, far_kind_hbm, basis_hbm, transfer_hbm,
+    table_hbm, parents_hbm, kinds_hbm,
+    out, xw, cw, blocks, up_out, up_in, near_out, near_in, total, own_near, fields, table16,
+    near_idx, far_idx, far_kind, kinds, basis, transfer, table, parents,
+    send, recv, local, staged,
 ):
     me, core = lax.axis_index("leaf"), lax.axis_index("cols")
     other = 1 - core
@@ -34,7 +36,7 @@
     far_slots = far_idx.shape[1]
     rows = basis.shape[2]
     half = near_hbm.shape[2]
-    cols = x_ref.shape[0]
+    cols = x_hbm.shape[0]
     depth = n.bit_length() - 1
     side = lax.rem(me, 2)
     pair = me + 1 - 2 * side
@@ -70,10 +72,29 @@
     def fetch(i):
         return pltpu.make_async_copy(near_hbm.at[i], blocks.at[i], local.at[i])
 
+    def own(i):
+        return pltpu.make_async_copy(
+            x_hbm.at[:, pl.ds(i * rows, rows)], xw.at[core, leaves + i], staged.at[i]
+        )
+
+    inputs = [
+        (basis_hbm, basis), (transfer_hbm, transfer), (parents_hbm, parents), (kinds_hbm, kinds),
+        (table_hbm, table), (far_idx_hbm, far_idx), (far_kind_hbm, far_kind),
+        (near_idx_hbm, near_idx),
+    ]
+    stages = [
+        pltpu.make_async_copy(src, dst, staged.at[leaves + j])
+        for j, (src, dst) in enumerate(inputs)
+    ]
+    for i in range(leaves):
+        own(i).start()
+    for stage in stages:
+        stage.start()
     for i in range(leaves):
         fetch(i).start()
-    for i in range(leaves):
-        xw[core, leaves + i] = x_ref[:, i * rows : (i + 1) * rows]
+    xw[0, 3 * leaves] = jnp.zeros((cols, rows), BF16)
+    xw[1, 3 * leaves] = jnp.zeros((cols, rows), BF16)
+    cw[3 * leaves] = jnp.zeros(cw.shape[1:], BF16)
 
     @pl.when(jnp.logical_not(has_source))
     def _():
@@ -81,6 +102,8 @@
         xw[1, pl.ds(relayed, leaves)] = jnp.zeros((leaves, cols, rows), BF16)
         cw[pl.ds(relayed, leaves)] = jnp.zeros((leaves,) + cw.shape[1:], BF16)
 
+    for i in range(leaves):
+        own(i).wait()
     peers = depth + has_onward.astype(jnp.int32) + has_source.astype(jnp.int32)
     pl.semaphore_wait(barrier, peers)
 
@@ -136,9 +159,11 @@
     for h in range(CHUNKS):
         across(0, leaves, h).start()
 
+    for stage in stages:
+        stage.wait()
     ancestor = jnp.zeros((cols, basis.shape[1]), F32)
     for i in range(leaves):
-        coef = nt(x_ref[:, i * rows : (i + 1) * rows], basis[i])
+        coef = nt(xw[core, leaves + i], basis[i])
         cw[leaves + i] = coef.astype(BF16)
         ancestor += nt(coef, transfer[i], HI)
     up_out[0] = ancestor
@@ -173,82 +198,86 @@
         def _():
             coef_from_relay.wait_recv()
 
-    tasks = [functools.partial(hand_on, h) for h in range(CHUNKS)]
-    tasks.insert(1, hand_coefs_on)
-    tasks += [functools.partial(pass_across, h) for h in range(CHUNKS)]
-    tasks.insert(4, coefs_in)
+    first = (me - 1) * leaves
+
+    def window(index):
+        inside = jnp.minimum(jnp.maximum(index - first, 0), 3 * leaves - 1)
+        return jnp.where(index >= 0, inside, 3 * leaves)
+
+    def far(i, carry):
+        field = jnp.zeros((cols, basis.shape[1]), F32)
+        for k in range(far_slots):
+            field += nt(cw[window(far_idx[i, k])], table16[far_kind[i, k]])
+        fields[i] = field
+        return carry
+
+    def far_part(low, high):
+        lax.fori_loop(low, high, far, 0, unroll=2)
+
+    tasks = [[functools.partial(hand_on, h)] for h in range(CHUNKS)]
+    tasks[0].append(hand_coefs_on)
+    tasks.append([functools.partial(pass_across, 0), coefs_in])
+    tasks[2].append(functools.partial(far_part, 0, leaves // 2))
+    tasks.append([functools.partial(pass_across, h) for h in range(1, CHUNKS)])
+    tasks[3].append(functools.partial(far_part, leaves // 2, leaves))
 
     couplings = []
     for level in range(depth):
+        child = lax.rem(me // (1 << level), 2)
+        ours = nt(ancestor, parents[child], HI)
+        for task in tasks.pop(0) if tasks else []:
+            task()
         up(level).wait_recv()
         sibling = up_in[level]
-        child = lax.rem(me // (1 << level), 2)
         if level + 1 < depth:
-            ancestor = nt(ancestor, parents[child], HI) + nt(sibling, parents[1 - child], HI)
+            ancestor = ours + nt(sibling, parents[1 - child], HI)
             up_out[level + 1] = ancestor
             up(level + 1).start()
-        if tasks:
-            tasks.pop(0)()
         number = (n // (2 << level)) + me // (2 << level)
         coupling = table[kinds[number - 1]]
         couplings.append(
             jnp.where(child == 0, nt(sibling, coupling, HI), nn(sibling, coupling, HI))
         )
+    for later in tasks:
+        for task in later:
+            task()
+
+    for h in range(CHUNKS):
+        from_across(0, leaves, h).wait_recv()
+        from_across(1, direct, h).wait_recv()
+
+    @pl.when(has_source)
+    def _():
+        for h in range(CHUNKS):
+            from_across(2, relayed, h).wait_recv()
+
+    for i in range(leaves):
+        fetch(i).wait()
+
+    def near(i, carry):
+        places = [window(near_idx[i, k]) for k in range(slots)]
+        block = jnp.concatenate([blocks[i, k] for k in range(slots)], axis=1)
+        theirs = jnp.concatenate([xw[other, p] for p in places], axis=1)
+        mine = jnp.concatenate([xw[core, p] for p in places], axis=1)
+        both = nt(jnp.concatenate([theirs, mine], axis=0), block)
+        near_out[i] = both[:cols]
+        near_copy(i).start()
+        own_near[i] = both[cols:]
+        return carry
+
+    lax.fori_loop(0, leaves, near, 0)
+
     down = couplings[depth - 1]
     for level in range(depth - 2, -1, -1):
         child = lax.rem(me // (1 << level), 2)
         down = nn(down, parents[child], HI) + couplings[level]
-    for task in tasks:
-        task()
-    first = (me - 1) * leaves
-
-    def window(index):
-        inside = jnp.minimum(jnp.maximum(index - first, 0), 3 * leaves - 1)
-        return jnp.where(index >= 0, inside, leaves)
-
-    def far(i, carry):
-        field = nn(down, transfer[i], HI)
-        for k in range(far_slots):
-            index = far_idx[i, k]
-            live = index >= 0
-            picked = cw[window(index)]
-            picked = jnp.where(live, picked, jnp.zeros_like(picked))
-            field += nt(picked, table16[far_kind[i, k]])
+
+    def expand(i, carry):
+        field = nn(down, transfer[i], HI) + fields[i]
         total[i] = nn(field.astype(BF16), basis[i])
         return carry
 
-    lax.fori_loop(0, leaves, far, 0)
-
-    for h in range(CHUNKS):
-        from_across(0, leaves, h).wait_recv()
-        from_across(1, direct, h).wait_recv()
-
-    @pl.when(has_source)
-    def _():
-        for h in range(CHUNKS):
-            from_across(2, relayed, h).wait_recv()
-
-    for i in range(leaves):
-        fetch(i).wait()
-
-    def near(i, carry):
-        mine = jnp.zeros((cols, half), F32)
-        theirs = jnp.zeros((cols, half), F32)
-        for k in range(slots):
-            index = near_idx[i, k]
-            live = index >= 0
-            place = window(index)
-            picked = jnp.concatenate([xw[core, place], xw[other, place]], axis=0)
-            picked = jnp.where(live, picked, jnp.zeros_like(picked))
-            both = nt(picked, blocks[i, k])
-            mine += both[:cols]
-            theirs += both[cols:]
-        near_out[i] = theirs
-        near_copy(i).start()
-        own_near[i] = mine
-        return carry
-
-    lax.fori_loop(0, leaves, near, 0)
+    lax.fori_loop(0, leaves, expand, 0, unroll=2)
 
     here = pl.multiple_of(core * half, half)
     across_half = pl.multiple_of(other * half, half)
@@ -295,16 +324,15 @@
     half = near_blocks.shape[2]
     copies = 5 * CHUNKS + 2 + depth + leaves
     vmem = pl.BlockSpec(memory_space=pltpu.VMEM)
-    smem = pl.BlockSpec(memory_space=pltpu.SMEM)
-    hbm = pl.BlockSpec(memory_space=pl.ANY)
+    hbm = pl.BlockSpec(memory_space=pltpu.HBM)
     return pl.pallas_call(
         functools.partial(kernel, n),
         out_shape=jax.ShapeDtypeStruct(vectors.shape, BF16),
-        in_specs=[vmem, hbm, smem, smem, smem, vmem, vmem, vmem, vmem, smem],
+        in_specs=[hbm] * 10,
         out_specs=vmem,
         scratch_shapes=[
-            pltpu.VMEM((2, 3 * leaves, cols, rows), BF16),
-            pltpu.VMEM((3 * leaves, cols, rank), BF16),
+            pltpu.VMEM((2, 3 * leaves + 1, cols, rows), BF16),
+            pltpu.VMEM((3 * leaves + 1, cols, rank), BF16),
             pltpu.VMEM(near_blocks.shape, BF16),
             pltpu.VMEM((depth, cols, rank), F32),
             pltpu.VMEM((depth, cols, rank), F32),
@@ -312,13 +340,23 @@
             pltpu.VMEM((leaves, cols, half), F32),
             pltpu.VMEM((leaves, cols, rows), F32),
             pltpu.VMEM((leaves, cols, half), F32),
+            pltpu.VMEM((leaves, cols, rank), F32),
             pltpu.VMEM(coupling_table.shape, BF16),
+            pltpu.SMEM(near_index.shape, jnp.int32),
+            pltpu.SMEM(far_index.shape, jnp.int32),
+            pltpu.SMEM(far_kind.shape, jnp.int32),
+            pltpu.SMEM(coarse_kind.shape, jnp.int32),
+            pltpu.VMEM(cluster_basis.shape, BF16),
+            pltpu.VMEM(leaf_transfer.shape, F32),
+            pltpu.VMEM(coupling_table.shape, F32),
+            pltpu.VMEM(parent_transfer_matrices.shape, F32),
             pltpu.SemaphoreType.DMA((copies,)),
             pltpu.SemaphoreType.DMA((copies,)),
             pltpu.SemaphoreType.DMA((leaves,)),
+            pltpu.SemaphoreType.DMA((leaves + 8,)),
         ],
         compiler_params=pltpu.CompilerParams(
-            collective_id=0, has_side_effects=True, vmem_limit_bytes=40 << 20
+            collective_id=0, has_side_effects=True, vmem_limit_bytes=60 << 20
         ),
         cost_estimate=pl.CostEstimate(flops=10**9, bytes_accessed=6 << 20, transcendentals=0),
     )(

time: 44.4 us -> 38.5 us (0.87)
  the two profiles are of different devices: /device:TPU:5 before, /device:TPU:0 now
where the time goes in v2:
time: 38.5 us; the launch traced here: 38.4 us
  Pallas kernels  36.7 us (95%)
  local copies, waits for them, and re-layouts  1.67 us (4%)
    pallas_call x1, Pallas kernels, shards(): pl.pallas_call(functools.partial(kernel, n), out_shape=jax.ShapeDtypeStru...  36.7 us
    unnamed x1, local copies, waits for them, and re-layouts  1.67 us

profile of v2, /device:TPU:0, one launch (start us, length us, event | category | flops | bytes accessed | tf_op | source)
XLA Modules:
  0.0 38.4 jit_solution(17856142811356059217)
XLA Ops:
  0.0 36.7 %shard_map.100 = bf16[64,2048]{1,0:T(8,128)(2,1)} custom-call(bf16[64,2048]{1,0:T(8,128)(2,1)} %x_hbm.1, bf16[8,8,128,256]{3,2,1,0:T(8,128)(2,1)} %near_hbm.1, s32[8,8]{1,0:T(8,128)} %near_idx_hbm.1, s32[8,8]{1,0:T(8,128)} %far_idx_hbm.1, s32[8,8]{1,0:T(8,128)} %far_kind_hbm.1, bf16[8,64,256]{2,1,0:T(8,128)(2,1)} %basis_hbm.1, f32[8,64,64]{2,1,0:T(8,128)} %transfer_hbm.1, ...), custom_call_target="tpu_custom_call" | custom-call | flops 1000000000 | bytes 6291456 | tf_op jit(solution)/shard_map/pallas_call | solution.py:328
  36.7 1.7 %copy.12 = bf16[64,2048]{1,0:T(8,128)(2,1)} copy(bf16[64,2048]{1,0:T(8,128)(2,1)} %shard_map.100) | data formatting | bytes 524288

commit v3 on v2

--- a/solution.py
+++ b/solution.py
@@ -154,11 +154,6 @@
     def near_copy(i):
         return copy(near_out.at[i], near_in.at[i], base + 2 + depth + i, me, other)
 
-    for h in range(CHUNKS):
-        to_pair(h).start()
-    for h in range(CHUNKS):
-        across(0, leaves, h).start()
-
     for stage in stages:
         stage.wait()
     ancestor = jnp.zeros((cols, basis.shape[1]), F32)
@@ -168,7 +163,12 @@
         ancestor += nt(coef, transfer[i], HI)
     up_out[0] = ancestor
     up(0).start()
-    coef_pair.start()
+    for h in range(CHUNKS):
+        to_pair(h).start()
+        if h == 0:
+            coef_pair.start()
+    for h in range(CHUNKS):
+        across(0, leaves, h).start()
     table16[...] = table[...].astype(BF16)
 
     def hand_on(h):
@@ -225,14 +225,14 @@
     for level in range(depth):
         child = lax.rem(me // (1 << level), 2)
         ours = nt(ancestor, parents[child], HI)
-        for task in tasks.pop(0) if tasks else []:
-            task()
         up(level).wait_recv()
         sibling = up_in[level]
         if level + 1 < depth:
             ancestor = ours + nt(sibling, parents[1 - child], HI)
             up_out[level + 1] = ancestor
             up(level + 1).start()
+        for task in tasks.pop(0) if tasks else []:
+            task()
         number = (n // (2 << level)) + me // (2 << level)
         coupling = table[kinds[number - 1]]
         couplings.append(

time: 38.5 us -> 32.6 us (0.85)
  the two profiles are of different devices: /device:TPU:0 before, /device:TPU:13 now
where the time goes in v3:
time: 32.6 us; the launch traced here: 32.5 us
  Pallas kernels  30.8 us (94%)
  local copies, waits for them, and re-layouts  1.67 us (5%)
    pallas_call x1, Pallas kernels, shards(): pl.pallas_call(functools.partial(kernel, n), out_shape=jax.ShapeDtypeStru...  30.8 us
    unnamed x1, local copies, waits for them, and re-layouts  1.67 us

profile of v3, /device:TPU:13, one launch (start us, length us, event | category | flops | bytes accessed | tf_op | source)
XLA Modules:
  0.0 32.5 jit_solution(17885040020727726221)
XLA Ops:
  0.0 30.8 %shard_map.100 = bf16[64,2048]{1,0:T(8,128)(2,1)} custom-call(bf16[64,2048]{1,0:T(8,128)(2,1)} %x_hbm.1, bf16[8,8,128,256]{3,2,1,0:T(8,128)(2,1)} %near_hbm.1, s32[8,8]{1,0:T(8,128)} %near_idx_hbm.1, s32[8,8]{1,0:T(8,128)} %far_idx_hbm.1, s32[8,8]{1,0:T(8,128)} %far_kind_hbm.1, bf16[8,64,256]{2,1,0:T(8,128)(2,1)} %basis_hbm.1, f32[8,64,64]{2,1,0:T(8,128)} %transfer_hbm.1, ...), custom_call_target="tpu_custom_call" | custom-call | flops 1000000000 | bytes 6291456 | tf_op jit(solution)/shard_map/pallas_call | solution.py:328
  30.8 1.7 %copy.12 = bf16[64,2048]{1,0:T(8,128)(2,1)} copy(bf16[64,2048]{1,0:T(8,128)(2,1)} %shard_map.100) | data formatting | bytes 524288

commit v4 on v3

--- a/solution.py
+++ b/solution.py
@@ -7,20 +7,32 @@
 from jax.experimental.pallas import tpu as pltpu
 from jax.sharding import PartitionSpec as P
 
-HI = lax.Precision.HIGHEST
 F32 = jnp.float32
 BF16 = jnp.bfloat16
 CHUNKS = 2
 
 
-def nt(a, b, precision=None):
-    return lax.dot_general(
-        a, b, (((1,), (1,)), ((), ())), precision=precision, preferred_element_type=F32
+def split(a):
+    high = a.astype(BF16)
+    return high, (a - high.astype(F32)).astype(BF16)
+
+
+def dot(a, b, dims, wide):
+    product = functools.partial(
+        lax.dot_general, dimension_numbers=(dims, ((), ())), preferred_element_type=F32
     )
-
-
-def nn(a, b, precision=None):
-    return jnp.dot(a, b, precision=precision, preferred_element_type=F32)
+    if not wide:
+        return product(a, b)
+    (a_high, a_low), (b_high, b_low) = split(a), split(b)
+    return product(a_high, b_high) + (product(a_high, b_low) + product(a_low, b_high))
+
+
+def nt(a, b, wide=False):
+    return dot(a, b, ((1,), (1,)), wide)
+
+
+def nn(a, b, wide=False):
+    return dot(a, b, ((1,), (0,)), wide)
 
 
 def kernel(
@@ -160,7 +172,7 @@
     for i in range(leaves):
         coef = nt(xw[core, leaves + i], basis[i])
         cw[leaves + i] = coef.astype(BF16)
-        ancestor += nt(coef, transfer[i], HI)
+        ancestor += nt(coef, transfer[i], True)
     up_out[0] = ancestor
     up(0).start()
     for h in range(CHUNKS):
@@ -216,19 +228,18 @@
 
     tasks = [[functools.partial(hand_on, h)] for h in range(CHUNKS)]
     tasks[0].append(hand_coefs_on)
-    tasks.append([functools.partial(pass_across, 0), coefs_in])
-    tasks[2].append(functools.partial(far_part, 0, leaves // 2))
+    tasks.append([functools.partial(pass_across, 0)])
     tasks.append([functools.partial(pass_across, h) for h in range(1, CHUNKS)])
-    tasks[3].append(functools.partial(far_part, leaves // 2, leaves))
+    tasks[3] += [coefs_in, functools.partial(far_part, 0, leaves)]
 
     couplings = []
     for level in range(depth):
         child = lax.rem(me // (1 << level), 2)
-        ours = nt(ancestor, parents[child], HI)
+        ours = nt(ancestor, parents[child], True)
         up(level).wait_recv()
         sibling = up_in[level]
         if level + 1 < depth:
-            ancestor = ours + nt(sibling, parents[1 - child], HI)
+            ancestor = ours + nt(sibling, parents[1 - child], True)
             up_out[level + 1] = ancestor
             up(level + 1).start()
         for task in tasks.pop(0) if tasks else []:
@@ -236,7 +247,7 @@
         number = (n // (2 << level)) + me // (2 << level)
         coupling = table[kinds[number - 1]]
         couplings.append(
-            jnp.where(child == 0, nt(sibling, coupling, HI), nn(sibling, coupling, HI))
+            jnp.where(child == 0, nt(sibling, coupling, True), nn(sibling, coupling, True))
         )
     for later in tasks:
         for task in later:
@@ -270,10 +281,10 @@
     down = couplings[depth - 1]
     for level in range(depth - 2, -1, -1):
         child = lax.rem(me // (1 << level), 2)
-        down = nn(down, parents[child], HI) + couplings[level]
+        down = nn(down, parents[child], True) + couplings[level]
 
     def expand(i, carry):
-        field = nn(down, transfer[i], HI) + fields[i]
+        field = nn(down, transfer[i], True) + fields[i]
         total[i] = nn(field.astype(BF16), basis[i])
         return carry
 

time: 32.6 us -> 31.8 us (0.975)
  Pallas kernels: 30.8 us -> 30 us
    pallas_call x1, Pallas kernels: 30.8 us -> 30 us  [shards(): pl.pallas_call(functools.partial(kernel, n), out_shape=jax.ShapeDtypeStru...]
where the time goes in v4:
time: 31.8 us; the launch traced here: 31.6 us
  Pallas kernels  30 us (94%)
  local copies, waits for them, and re-layouts  1.67 us (5%)
    pallas_call x1, Pallas kernels, shards(): pl.pallas_call(functools.partial(kernel, n), out_shape=jax.ShapeDtypeStru...  30 us
    unnamed x1, local copies, waits for them, and re-layouts  1.67 us

profile of v4, /device:TPU:13, one launch (start us, length us, event | category | flops | bytes accessed | tf_op | source)
XLA Modules:
  0.0 31.6 jit_solution(17145808492745436388)
XLA Ops:
  0.0 30.0 %shard_map.100 = bf16[64,2048]{1,0:T(8,128)(2,1)} custom-call(bf16[64,2048]{1,0:T(8,128)(2,1)} %x_hbm.1, bf16[8,8,128,256]{3,2,1,0:T(8,128)(2,1)} %near_hbm.1, s32[8,8]{1,0:T(8,128)} %near_idx_hbm.1, s32[8,8]{1,0:T(8,128)} %far_idx_hbm.1, s32[8,8]{1,0:T(8,128)} %far_kind_hbm.1, bf16[8,64,256]{2,1,0:T(8,128)(2,1)} %basis_hbm.1, f32[8,64,64]{2,1,0:T(8,128)} %transfer_hbm.1, ...), custom_call_target="tpu_custom_call" | custom-call | flops 1000000000 | bytes 6291456 | tf_op jit(solution)/shard_map/pallas_call | solution.py:339
  30.0 1.7 %copy.12 = bf16[64,2048]{1,0:T(8,128)(2,1)} copy(bf16[64,2048]{1,0:T(8,128)(2,1)} %shard_map.100) | data formatting | bytes 524288
